TPU v7x, 32 devices: a whole 2x2x4 slice. The times are simulated.
32 devices in a mesh: gx: 4 (over y, x), gy: 8 (over z, core).
Axes of the slice: x: 2, y: 2, z: 4, core: 2. Of those that a mesh axis runs over, the one named last changes fastest.
Arguments:
- particles: float32 [4, 8, 32, 6, 128], P('gx', 'gy'), may hold values from -5 to 5, as said below
- dinv: float32 [4, 8, 32, 128, 128], P('gx', 'gy'), may hold values from -2 to 2
- low_bound: float32 [1], replicated, may hold values from 0.3 to 0.6
- high_bound: float32 [1], replicated, may hold values from 2.2 to 3.2
- counts: int32 [4, 8], P('gx', 'gy'), may hold values from 24 to 32, as said below
- send_list: int32 [4, 8, 24], P('gx', 'gy'), may hold values from 0 to 31, as said below
- nbr_dir: int32 [4, 8, 32, 9], P('gx', 'gy'), may hold values from 0 to 8, as said below
- nbr_slot: int32 [4, 8, 32, 9], P('gx', 'gy'), may hold values from 0 to 31, as said below
Outputs:
- pressure: float32 [4, 8, 32, 128], P('gx', 'gy')
- velocity: float32 [4, 8, 32, 3, 128], P('gx', 'gy')
Inputs may be any that keep to these rules, and one draw needn't show every extreme that they name: `counts`: device (0, 0) has all 32 slots live; live tiles fill the lowest slots. `send_list`: 24 distinct live slots of the device. `nbr_dir`: entry 0 of every tile is 4 (its own device). Other codes name only devices that exist. `nbr_slot`: entry 0 is the tile's own slot. For code 4 other entries are live slots of the device; for other codes, positions below 24 in the owner's send_list. `particles`: positions lie in [0, 1).
All inputs are finite; a program needn't handle non-finite values.
Results may differ from a plain program's by a relative error of at most 0.0003.
Values sent between devices are 32-bit elements; how exact they have to be, the bound alone decides.
A program may use at most 128 MiB of HBM per device.

v0:
```python
import functools

import jax
import jax.numpy as jnp
from jax import lax
from jax.experimental import pallas as pl
from jax.experimental.pallas import tpu as pltpu
from jax.sharding import PartitionSpec as P

ITERS = 3
MESH = pl.DeviceIdType.MESH
CODES = (0, 1, 2, 3, 5, 6, 7, 8)
F32 = jnp.float32
BF16 = jnp.bfloat16


def split(value):
    head = value.astype(BF16).astype(F32)
    return jnp.concatenate([head, value - head], axis=0).astype(BF16)


def split_row(row):
    wide = jnp.broadcast_to(row, (8, row.shape[1]))
    head = wide.astype(BF16).astype(F32)
    first = lax.broadcasted_iota(jnp.int32, wide.shape, 0) == 0
    return jnp.where(first, head, wide - head).astype(BF16)


def kernel(px, py, sizes, part_ref, dinv_ref, low_ref, high_ref, counts_ref, send_ref, dir_ref, slot_ref,
           press_ref, vel_ref,
           w, draw, dinv_t, pos, mot, flow, flow_own, step0, step1, step2, step_own, total_p, sums, src, ztot, mres,
           st_pos, st_mot, st_flow, st_step0, st_step1, st_step2, dsem, send_sem, recv_sem):
    S, G, K, T = sizes
    steps = (step0, step1, step2)
    st_step = (st_step0, st_step1, st_step2)
    i = lax.axis_index("gx")
    j = lax.axis_index("gy")

    def inside(di, dj):
        return (i + di >= 0) & (i + di < px) & (j + dj >= 0) & (j + dj < py)

    barrier = pltpu.get_barrier_semaphore()
    straight = ((-1, 0), (1, 0), (0, -1), (0, 1))
    for di, dj in straight:
        @pl.when(inside(di, dj))
        def _():
            pl.semaphore_signal(barrier, inc=1, device_id=(i + di, j + dj), device_id_type=MESH)

    load_dinv = pltpu.make_async_copy(dinv_ref.at[0, 0], draw, dsem)
    load_dinv.start()

    def make_tile(s):
        block = part_ref[0, 0, s]
        place = 2.0 * block[0:3] - 1.0
        square = place * place
        norm = -(square[0:1] + square[1:2] + square[2:3])
        return (jnp.concatenate([place, norm], axis=0),
                jnp.concatenate([block[3:6], jnp.ones((1, T), F32)], axis=0))

    def stage_tile(g, _):
        st_pos[g], st_mot[g] = make_tile(send_ref[0, 0, g])
        return 0

    lax.fori_loop(0, G, stage_tile, 0, unroll=4)
    pl.semaphore_wait(barrier, sum(inside(di, dj).astype(jnp.int32) for di, dj in straight))

    def ghosts(ext, code):
        return ext.at[pl.ds(S + code * G, G)]

    def transfer(e, ext, source, code):
        di, dj = code // 3 - 1, code % 3 - 1
        if di != 0 and dj != 0:
            source = ghosts(ext, 3 * (di + 1) + 1)
            target = (i, j - dj)
        else:
            target = (i - di, j - dj)
        return pltpu.make_async_remote_copy(
            src_ref=source, dst_ref=ghosts(ext, code), send_sem=send_sem.at[e, code],
            recv_sem=recv_sem.at[e, code], device_id=target, device_id_type=MESH)

    def sends(code):
        di, dj = code // 3 - 1, code % 3 - 1
        if di != 0 and dj != 0:
            return inside(di, 0) & inside(0, -dj)
        return inside(-di, -dj)

    def begin(e, ext, staged):
        for code in (1, 7, 3, 5):
            @pl.when(sends(code))
            def _():
                transfer(e, ext, staged, code).start()

    def forward(e, ext, staged):
        for code in (1, 7):
            @pl.when(inside(code // 3 - 1, 0))
            def _():
                transfer(e, ext, staged, code).wait_recv()
            for follow in (code - 1, code + 1):
                @pl.when(sends(follow))
                def _():
                    transfer(e, ext, staged, follow).start()

    def arrive(e, ext, staged):
        for code in (3, 5, 0, 2, 6, 8):
            @pl.when(inside(code // 3 - 1, code % 3 - 1))
            def _():
                transfer(e, ext, staged, code).wait_recv()

    def finish(e, ext, staged):
        for code in CODES:
            @pl.when(sends(code))
            def _():
                transfer(e, ext, staged, code).wait_send()

    begin(0, pos, st_pos)
    begin(1, mot, st_mot)

    def own_tile(s, _):
        pos[s], mot[s] = make_tile(s)
        return 0

    lax.fori_loop(0, S, own_tile, 0, unroll=4)
    load_dinv.wait()
    forward(0, pos, st_pos)
    forward(1, mot, st_mot)

    def turn(s, _):
        dinv_t[s] = split(draw[s].T)
        return 0

    lax.fori_loop(0, S, turn, 0, unroll=2)
    arrive(0, pos, st_pos)

    def neighbour(s, k):
        code = dir_ref[0, 0, s, k]
        slot = slot_ref[0, 0, s, k]
        return jnp.where(code == 4, slot, S + code * G + slot)

    row4 = lax.broadcasted_iota(jnp.int32, (4, T), 0)
    unit4 = jnp.where(row4 == 0, 1.0, 0.0)

    def weigh(s, _):
        own = pos[s]
        own_rows = jnp.concatenate([jnp.where(row4 == 3, 1.0, 2.0 * own), jnp.where(row4 == 0, 1.0 + own[3:4], 0.0)], axis=0)
        head = own_rows.astype(BF16).astype(F32)
        rest = own_rows - head
        own_side = jnp.concatenate([head, head, rest, rest], axis=0).astype(BF16)
        for k in range(K):
            near = split(jnp.concatenate([pos[neighbour(s, k)], unit4], axis=0))
            near_side = jnp.concatenate([near, near], axis=0)
            value = lax.dot_general(near_side, own_side, (((0,), (0,)), ((), ())), preferred_element_type=F32)
            value = jnp.maximum(value, 0.0)
            value = value * value * value
            top = value.astype(BF16)
            w[s, 2 * k * T:(2 * k + 1) * T, :] = top
            w[s, (2 * k + 1) * T:(2 * k + 2) * T, :] = (value - top.astype(F32)).astype(BF16)
        return 0

    lax.fori_loop(0, S, weigh, 0, unroll=2)
    arrive(1, mot, st_mot)

    def apply(s, feature):
        parts = []
        for k in range(K):
            part = feature(neighbour(s, k))
            parts += [part, part]
        return jnp.dot(jnp.concatenate(parts, axis=1), w[s], preferred_element_type=F32)

    def viscous(s, _):
        out = apply(s, lambda n: split(jnp.concatenate([pos[n], mot[n]], axis=0)))
        out = out[0:8] + out[8:16]
        sums[s] = out
        speed = mot[s]
        ustar = speed + 0.5 * (out[4:8] / out[7:8] - speed)
        both = pos[s] * ustar
        rows = jnp.concatenate([ustar[0:3], both[0:1] + both[1:2] + both[2:3]], axis=0)
        flow[s] = rows
        flow_own[s] = rows
        return 0

    lax.fori_loop(0, S, viscous, 0, unroll=4)

    def stage_flow(g, _):
        st_flow[g] = flow_own[send_ref[0, 0, g]]
        return 0

    def exchange(e, ext, staged):
        begin(e, ext, staged)
        forward(e, ext, staged)
        arrive(e, ext, staged)

    lax.fori_loop(0, G, stage_flow, 0, unroll=8)
    exchange(2, flow, st_flow)

    def source(s, _):
        out = apply(s, lambda n: split(flow[n]))
        out = out[0:4] + out[4:8]
        known = sums[s]
        place = pos[s]
        own = flow[s]
        total = known[7:8]
        cross = place * out + own * known[0:4]
        value = total * own[3:4] - (cross[0:1] + cross[1:2] + cross[2:3]) + out[3:4]
        src[pl.ds(s, 1), :] = 4.0 * value / total
        ztot[pl.ds(s, 1), :] = total
        return 0

    lax.fori_loop(0, S, source, 0, unroll=4)

    def precondition():
        def one(s, _):
            row = split_row(src[pl.ds(s, 1), :])
            out = jnp.dot(jnp.concatenate([row, row], axis=1), dinv_t[s], preferred_element_type=F32)
            mres[pl.ds(s, 1), :] = out[0:1] + out[1:2]
            return 0

        lax.fori_loop(0, S, one, 0, unroll=8)
        return mres[...]

    low = jnp.full((1, T), low_ref[0], F32)
    high = jnp.full((1, T), high_ref[0], F32)
    theta = (high + low) / 2.0
    delta = (high - low) / 2.0
    sigma = theta / delta
    rho = 1.0 / sigma
    step = precondition() / theta
    for it in range(ITERS):
        ext = steps[it]
        staged = st_step[it]
        ext[0:S] = step
        step_own[...] = step

        def stage_step(g, _):
            staged[pl.ds(g, 1), :] = step_own[pl.ds(send_ref[0, 0, g], 1), :]
            return 0

        lax.fori_loop(0, G, stage_step, 0, unroll=8)
        exchange(3 + it, ext, staged)
        if it + 1 < ITERS:
            def operate(s, _):
                out = apply(s, lambda n: split_row(ext[pl.ds(n, 1), :]))
                mres[pl.ds(s, 1), :] = out[0:1] + out[1:2]
                return 0

            lax.fori_loop(0, S, operate, 0, unroll=4)
            src[...] = src[...] - (2.0 * step - mres[...] / ztot[...])
            rho_new = 1.0 / (2.0 * sigma - rho)
            step = rho_new * rho * step + 2.0 * rho_new / delta * precondition()
            rho = rho_new

    total_p[...] = step0[...] + step1[...] + step2[...]
    count = counts_ref[0, 0]
    live = lax.broadcasted_iota(jnp.int32, (S, T), 0) < count
    press_ref[0, 0] = jnp.where(live, total_p[0:S], 0.0)

    def gradient(s, _):
        def feature(n):
            return split(jnp.where(row4 == 3, 1.0, pos[n]) * total_p[pl.ds(n, 1), :])

        out = apply(s, feature)
        out = out[0:4] + out[4:8]
        known = sums[s]
        place = pos[s]
        own_p = total_p[pl.ds(s, 1), :]
        total = known[7:8]
        value = out - place * out[3:4] - own_p * known[0:4] + own_p * place * total
        result = flow[s] - 2.0 * (value / total)
        alive = jnp.full((3, T), count, jnp.int32) > s
        vel_ref[0, 0, s] = jnp.where(alive, result[0:3], 0.0)
        return 0

    lax.fori_loop(0, S, gradient, 0, unroll=4)

    finish(0, pos, st_pos)
    finish(1, mot, st_mot)
    finish(2, flow, st_flow)
    for it in range(ITERS):
        finish(3 + it, steps[it], st_step[it])


def body(px, py, particles, dinv, low_bound, high_bound, counts, send_list, nbr_dir, nbr_slot):
    S, T = particles.shape[2], particles.shape[4]
    G = send_list.shape[2]
    K = nbr_dir.shape[3]
    N = S + 9 * G
    vmem = pl.BlockSpec(memory_space=pltpu.VMEM)
    smem = pl.BlockSpec(memory_space=pltpu.SMEM)
    exchanges = 3 + ITERS
    return pl.pallas_call(
        functools.partial(kernel, px, py, (S, G, K, T)),
        out_shape=(jax.ShapeDtypeStruct((1, 1, S, T), F32), jax.ShapeDtypeStruct((1, 1, S, 3, T), F32)),
        in_specs=[vmem, pl.BlockSpec(memory_space=pl.ANY), smem, smem, smem, smem, smem, smem],
        out_specs=(vmem, vmem),
        scratch_shapes=[
            pltpu.VMEM((S, 2 * K * T, T), BF16),
            pltpu.VMEM((S, T, T), F32),
            pltpu.VMEM((S, 2 * T, T), BF16),
            pltpu.VMEM((N, 4, T), F32),
            pltpu.VMEM((N, 4, T), F32),
            pltpu.VMEM((N, 4, T), F32),
            pltpu.VMEM((S, 4, T), F32),
            *[pltpu.VMEM((N, T), F32)] * ITERS,
            pltpu.VMEM((S, T), F32),
            pltpu.VMEM((N, T), F32),
            pltpu.VMEM((S, 8, T), F32),
            pltpu.VMEM((S, T), F32),
            pltpu.VMEM((S, T), F32),
            pltpu.VMEM((S, T), F32),
            pltpu.VMEM((G, 4, T), F32),
            pltpu.VMEM((G, 4, T), F32),
            pltpu.VMEM((G, 4, T), F32),
            *[pltpu.VMEM((G, T), F32)] * ITERS,
            pltpu.SemaphoreType.DMA,
            pltpu.SemaphoreType.DMA((exchanges, 9)),
            pltpu.SemaphoreType.DMA((exchanges, 9)),
        ],
        compiler_params=pltpu.CompilerParams(
            collective_id=0, has_side_effects=True, vmem_limit_bytes=48 << 20),
    )(particles, dinv, low_bound, high_bound, counts, send_list, nbr_dir, nbr_slot)


def solution(mesh):
    placed = (
        P("gx", "gy", None, None, None),
        P("gx", "gy", None, None, None),
        P(),
        P(),
        P("gx", "gy"),
        P("gx", "gy", None),
        P("gx", "gy", None, None),
        P("gx", "gy", None, None),
    )
    return jax.shard_map(
        functools.partial(body, mesh.shape["gx"], mesh.shape["gy"]),
        mesh=mesh,
        in_specs=placed,
        out_specs=(P("gx", "gy", None, None), P("gx", "gy", None, None, None)),
        check_vma=False,
    )
```

profile of v0, /device:TPU:1, one launch (start us, length us, event | category | flops | bytes accessed | tf_op | source)
XLA Modules:
  0.0 70.7 jit_solution(9631212878761945343)
XLA Ops:
  2.6 0.8 %copy.11.dir_ref = s32[1,1,32,9]{3,2,1,0:T(8,128)S(1)} copy(s32[1,1,32,9]{2,1,3,0:T(1,128)} %param.14) | data formatting | bytes 2304 | tf_op args[6]
  3.3 0.8 %copy.12.slot_ref = s32[1,1,32,9]{3,2,1,0:T(8,128)S(1)} copy(s32[1,1,32,9]{2,1,3,0:T(1,128)} %param.15) | data formatting | bytes 2304 | tf_op args[7]
  4.1 1.0 %copy.10.part_ref = f32[1,1,32,6,128]{4,3,2,1,0:T(8,128)S(1)} copy(f32[1,1,32,6,128]{4,2,3,1,0:T(8,128)} %param.8) | data formatting | bytes 196608 | tf_op args[0]
  5.1 0.0 copy-start
  5.1 1.6 %copy-done = f32[1,1,32,128,128]{4,3,2,1,0:T(8,128)S(1)} copy-done((f32[1,1,32,128,128]{4,3,2,1,0:T(8,128)S(1)}, f32[1,1,32,128,128]{4,3,2,1,0:T(8,128)}, u32[]{:S(2)}) %copy-start) | copy-done | bytes 2097176
  6.7 0.0 copy-start.1
  6.7 0.7 copy-done.1
  7.3 62.1 %shard_map.95 = (f32[1,1,32,128]{3,2,1,0:T(8,128)S(1)}, f32[1,1,32,3,128]{4,3,2,1,0:T(4,128)S(1)}) custom-call(f32[1,1,32,6,128]{4,3,2,1,0:T(8,128)S(1)} %copy.10.part_ref, f32[1,1,32,128,128]{4,3,2,1,0:T(8,128)S(1)} %copy-done, f32[1]{0:T(128)S(6)} %copy.15.low_ref, f32[1]{0:T(128)S(6)} %copy.16.high_ref, s32[1,1]{1,0:T(1,128)S(6)} %copy.17.counts_ref, ...), custom_call_target="tpu_custom_call" | custom-call | tf_op jit(solution)/shard_map/pallas_call | solution.py:289
  69.5 0.6 copy.13
  70.1 0.6 copy.18
Async XLA Ops:
  5.1 1.6 %copy-start = (f32[1,1,32,128,128]{4,3,2,1,0:T(8,128)S(1)}, f32[1,1,32,128,128]{4,3,2,1,0:T(8,128)}, u32[]{:S(2)}) copy-start(f32[1,1,32,128,128]{4,3,2,1,0:T(8,128)} %dinv_ref.1) | copy-start | bytes 6291460
  6.7 0.7 copy-start.1
where the time goes:
time: 71 us; the launch traced here: 70.7 us
  Pallas kernels  62.1 us (87%)
  local copies, waits for them, and re-layouts  5.96 us (8%)
  between operations  2.59 us (4%)
    pallas_call x1, Pallas kernels, body(): pl.pallas_call(functools.partial(kernel, px, py, (S, G, K, T)), out_shape...  62.1 us
    unnamed x8, local copies, waits for them, and re-layouts  5.33 us

commit v1 on v0

--- a/solution.py
+++ b/solution.py
@@ -9,6 +9,7 @@
 
 ITERS = 3
 MESH = pl.DeviceIdType.MESH
+DIRECT = (3, 4, 5)
 CODES = (0, 1, 2, 3, 5, 6, 7, 8)
 F32 = jnp.float32
 BF16 = jnp.bfloat16
@@ -40,7 +41,7 @@
         return (i + di >= 0) & (i + di < px) & (j + dj >= 0) & (j + dj < py)
 
     barrier = pltpu.get_barrier_semaphore()
-    straight = ((-1, 0), (1, 0), (0, -1), (0, 1))
+    straight = tuple((c // 3 - 1, c % 3 - 1) for c in CODES)
     for di, dj in straight:
         @pl.when(inside(di, dj))
         def _():
@@ -50,12 +51,11 @@
     load_dinv.start()
 
     def make_tile(s):
-        block = part_ref[0, 0, s]
-        place = 2.0 * block[0:3] - 1.0
-        square = place * place
-        norm = -(square[0:1] + square[1:2] + square[2:3])
-        return (jnp.concatenate([place, norm], axis=0),
-                jnp.concatenate([block[3:6], jnp.ones((1, T), F32)], axis=0))
+        rows = [part_ref[0, 0, c, pl.ds(s, 1), :] for c in range(6)]
+        place = [2.0 * row - 1.0 for row in rows[:3]]
+        norm = -(place[0] * place[0] + place[1] * place[1] + place[2] * place[2])
+        return (jnp.concatenate(place + [norm], axis=0),
+                jnp.concatenate(rows[3:] + [jnp.ones((1, T), F32)], axis=0))
 
     def stage_tile(g, _):
         st_pos[g], st_mot[g] = make_tile(send_ref[0, 0, g])
@@ -69,7 +69,7 @@
 
     def transfer(e, ext, source, code):
         di, dj = code // 3 - 1, code % 3 - 1
-        if di != 0 and dj != 0:
+        if di != 0 and dj != 0 and e not in DIRECT:
             source = ghosts(ext, 3 * (di + 1) + 1)
             target = (i, j - dj)
         else:
@@ -78,37 +78,39 @@
             src_ref=source, dst_ref=ghosts(ext, code), send_sem=send_sem.at[e, code],
             recv_sem=recv_sem.at[e, code], device_id=target, device_id_type=MESH)
 
-    def sends(code):
+    def sends(e, code):
         di, dj = code // 3 - 1, code % 3 - 1
-        if di != 0 and dj != 0:
+        if di != 0 and dj != 0 and e not in DIRECT:
             return inside(di, 0) & inside(0, -dj)
         return inside(-di, -dj)
 
     def begin(e, ext, staged):
-        for code in (1, 7, 3, 5):
-            @pl.when(sends(code))
+        for code in (0, 2, 6, 8, 1, 7, 3, 5) if e in DIRECT else (1, 7, 3, 5):
+            @pl.when(sends(e, code))
             def _():
                 transfer(e, ext, staged, code).start()
 
     def forward(e, ext, staged):
+        if e in DIRECT:
+            return
         for code in (1, 7):
             @pl.when(inside(code // 3 - 1, 0))
             def _():
                 transfer(e, ext, staged, code).wait_recv()
             for follow in (code - 1, code + 1):
-                @pl.when(sends(follow))
+                @pl.when(sends(e, follow))
                 def _():
                     transfer(e, ext, staged, follow).start()
 
     def arrive(e, ext, staged):
-        for code in (3, 5, 0, 2, 6, 8):
+        for code in CODES if e in DIRECT else (3, 5, 0, 2, 6, 8):
             @pl.when(inside(code // 3 - 1, code % 3 - 1))
             def _():
                 transfer(e, ext, staged, code).wait_recv()
 
     def finish(e, ext, staged):
         for code in CODES:
-            @pl.when(sends(code))
+            @pl.when(sends(e, code))
             def _():
                 transfer(e, ext, staged, code).wait_send()
 
@@ -120,20 +122,20 @@
         return 0
 
     lax.fori_loop(0, S, own_tile, 0, unroll=4)
+    forward(0, pos, st_pos)
     load_dinv.wait()
-    forward(0, pos, st_pos)
-    forward(1, mot, st_mot)
 
     def turn(s, _):
         dinv_t[s] = split(draw[s].T)
         return 0
 
     lax.fori_loop(0, S, turn, 0, unroll=2)
+    forward(1, mot, st_mot)
     arrive(0, pos, st_pos)
 
     def neighbour(s, k):
-        code = dir_ref[0, 0, s, k]
-        slot = slot_ref[0, 0, s, k]
+        code = dir_ref[0, 0, k, s]
+        slot = slot_ref[0, 0, k, s]
         return jnp.where(code == 4, slot, S + code * G + slot)
 
     row4 = lax.broadcasted_iota(jnp.int32, (4, T), 0)
@@ -156,7 +158,7 @@
             w[s, (2 * k + 1) * T:(2 * k + 2) * T, :] = (value - top.astype(F32)).astype(BF16)
         return 0
 
-    lax.fori_loop(0, S, weigh, 0, unroll=2)
+    lax.fori_loop(0, S, weigh, 0, unroll=4)
     arrive(1, mot, st_mot)
 
     def apply(s, feature):
@@ -266,7 +268,9 @@
         value = out - place * out[3:4] - own_p * known[0:4] + own_p * place * total
         result = flow[s] - 2.0 * (value / total)
         alive = jnp.full((3, T), count, jnp.int32) > s
-        vel_ref[0, 0, s] = jnp.where(alive, result[0:3], 0.0)
+        result = jnp.where(alive, result[0:3], 0.0)
+        for c in range(3):
+            vel_ref[0, 0, c, pl.ds(s, 1), :] = result[c:c + 1]
         return 0
 
     lax.fori_loop(0, S, gradient, 0, unroll=4)
@@ -286,10 +290,11 @@
     vmem = pl.BlockSpec(memory_space=pltpu.VMEM)
     smem = pl.BlockSpec(memory_space=pltpu.SMEM)
     exchanges = 3 + ITERS
-    return pl.pallas_call(
+    swap = lambda array: jnp.swapaxes(array, 2, 3)
+    press, vel = pl.pallas_call(
         functools.partial(kernel, px, py, (S, G, K, T)),
-        out_shape=(jax.ShapeDtypeStruct((1, 1, S, T), F32), jax.ShapeDtypeStruct((1, 1, S, 3, T), F32)),
-        in_specs=[vmem, pl.BlockSpec(memory_space=pl.ANY), smem, smem, smem, smem, smem, smem],
+        out_shape=(jax.ShapeDtypeStruct((1, 1, S, T), F32), jax.ShapeDtypeStruct((1, 1, 3, S, T), F32)),
+        in_specs=[vmem, pl.BlockSpec(memory_space=pltpu.HBM), smem, smem, smem, smem, smem, smem],
         out_specs=(vmem, vmem),
         scratch_shapes=[
             pltpu.VMEM((S, 2 * K * T, T), BF16),
@@ -316,7 +321,8 @@
         ],
         compiler_params=pltpu.CompilerParams(
             collective_id=0, has_side_effects=True, vmem_limit_bytes=48 << 20),
-    )(particles, dinv, low_bound, high_bound, counts, send_list, nbr_dir, nbr_slot)
+    )(swap(particles), dinv, low_bound, high_bound, counts, send_list, swap(nbr_dir), swap(nbr_slot))
+    return press, swap(vel)
 
 
 def solution(mesh):

time: 71 us -> 63.6 us (0.90)
  Pallas kernels: 62.1 us -> 55.2 us
  local copies, waits for them, and re-layouts: 5.96 us -> 5.07 us
    pallas_call x1, Pallas kernels: 62.1 us -> 55.2 us  [body(): pl.pallas_call(functools.partial(kernel, px, py, (S, G, K, T)), out_shape...]
    unnamed x8, local copies, waits for them, and re-layouts: 5.33 us -> 4.36 us
where the time goes in v1:
time: 63.6 us; the launch traced here: 62.9 us
  Pallas kernels  55.2 us (87%)
  local copies, waits for them, and re-layouts  5.07 us (8%)
  between operations  2.58 us (4%)
    pallas_call x1, Pallas kernels, body(): pl.pallas_call(functools.partial(kernel, px, py, (S, G, K, T)), out_shape...  55.2 us
    unnamed x8, local copies, waits for them, and re-layouts  4.36 us

profile of v1, /device:TPU:1, one launch (start us, length us, event | category | flops | bytes accessed | tf_op | source)
XLA Modules:
  0.0 62.9 jit_solution(5049351184345586568)
XLA Ops:
  2.6 0.7 %copy_bitcast_fusion = (s32[1,1,9,32]{3,2,1,0:T(8,128)S(1)}, s32[1,1,9,32]{3,2,1,0:T(8,128)S(1)}) fusion(s32[1,1,32,9]{2,1,3,0:T(1,128)} %param.15, s32[1,1,32,9]{2,1,3,0:T(1,128)} %param.14), kind=kLoop, calls=%fused_computation | loop fusion | bytes 4608 | tf_op jit(solution)/shard_map/transpose | solution.py:293
  3.3 0.0 copy-start
  3.3 1.6 %copy-done = f32[1,1,32,128,128]{4,3,2,1,0:T(8,128)S(1)} copy-done((f32[1,1,32,128,128]{4,3,2,1,0:T(8,128)S(1)}, f32[1,1,32,128,128]{4,3,2,1,0:T(8,128)}, u32[]{:S(2)}) %copy-start) | copy-done | bytes 2097176
  4.9 0.0 copy-start.1
  4.9 0.9 %copy-done.1 = f32[1,1,32,6,128]{4,2,3,1,0:T(8,128)S(1)} copy-done((f32[1,1,32,6,128]{4,2,3,1,0:T(8,128)S(1)}, f32[1,1,32,6,128]{4,2,3,1,0:T(8,128)}, u32[]{:S(2)}) %copy-start.1) | copy-done | bytes 98328
  5.8 0.0 copy-start.2
  5.8 0.7 %copy-done.2 = s32[1,1,24]{2,1,0:T(1,128)S(1)} copy-done((s32[1,1,24]{2,1,0:T(1,128)S(1)}, s32[1,1,24]{2,1,0:T(1,128)}, u32[]{:S(2)}) %copy-start.2) | copy-done | bytes 120
  6.4 55.2 %shard_map.95 = (f32[1,1,32,128]{3,2,1,0:T(8,128)S(1)}, f32[1,1,3,32,128]{4,3,2,1,0:T(8,128)S(1)}) custom-call(f32[1,1,6,32,128]{4,3,2,1,0:T(8,128)S(1)} %bitcast.6, f32[1,1,32,128,128]{4,3,2,1,0:T(8,128)S(1)} %copy-done, f32[1]{0:T(128)S(6)} %copy.16.low_ref, f32[1]{0:T(128)S(6)} %copy.17.high_ref, s32[1,1]{1,0:T(1,128)S(6)} %copy.18.counts_ref, ...), custom_call_target="tpu_custom_call" | custom-call | tf_op jit(solution)/shard_map/pallas_call | solution.py:294
  61.6 0.6 copy.19
  62.2 0.6 copy.20
Async XLA Ops:
  3.3 1.6 %copy-start = (f32[1,1,32,128,128]{4,3,2,1,0:T(8,128)S(1)}, f32[1,1,32,128,128]{4,3,2,1,0:T(8,128)}, u32[]{:S(2)}) copy-start(f32[1,1,32,128,128]{4,3,2,1,0:T(8,128)} %dinv_ref.1) | copy-start | bytes 6291460
  4.9 0.9 %copy-start.1 = (f32[1,1,32,6,128]{4,2,3,1,0:T(8,128)S(1)}, f32[1,1,32,6,128]{4,2,3,1,0:T(8,128)}, u32[]{:S(2)}) copy-start(f32[1,1,32,6,128]{4,2,3,1,0:T(8,128)} %param.8) | copy-start | bytes 294916
  5.8 0.7 %copy-start.2 = (s32[1,1,24]{2,1,0:T(1,128)S(1)}, s32[1,1,24]{2,1,0:T(1,128)}, u32[]{:S(2)}) copy-start(s32[1,1,24]{2,1,0:T(1,128)} %send_ref.1) | copy-start | bytes 292

commit v2 on v1

--- a/solution.py
+++ b/solution.py
@@ -10,6 +10,7 @@
 ITERS = 3
 MESH = pl.DeviceIdType.MESH
 DIRECT = (3, 4, 5)
+LATE = 6
 CODES = (0, 1, 2, 3, 5, 6, 7, 8)
 F32 = jnp.float32
 BF16 = jnp.bfloat16
@@ -29,8 +30,8 @@
 
 def kernel(px, py, sizes, part_ref, dinv_ref, low_ref, high_ref, counts_ref, send_ref, dir_ref, slot_ref,
            press_ref, vel_ref,
-           w, draw, dinv_t, pos, mot, flow, flow_own, step0, step1, step2, step_own, total_p, sums, src, ztot, mres,
-           st_pos, st_mot, st_flow, st_step0, st_step1, st_step2, dsem, send_sem, recv_sem):
+           w, draw, dinv_t, pos, mot, flow, step0, step1, step2, step_own, total_p, sums, src, ztot, mres,
+           st_pos, st_mot, st_flow, st_late, st_step0, st_step1, st_step2, dsem, send_sem, recv_sem):
     S, G, K, T = sizes
     steps = (step0, step1, step2)
     st_step = (st_step0, st_step1, st_step2)
@@ -64,18 +65,24 @@
     lax.fori_loop(0, G, stage_tile, 0, unroll=4)
     pl.semaphore_wait(barrier, sum(inside(di, dj).astype(jnp.int32) for di, dj in straight))
 
-    def ghosts(ext, code):
+    half = G // 2
+
+    def ghosts(e, ext, code):
+        if e == 2:
+            return ext.at[pl.ds(S + code * G, half)]
+        if e == LATE:
+            return ext.at[pl.ds(S + code * G + half, G - half)]
         return ext.at[pl.ds(S + code * G, G)]
 
     def transfer(e, ext, source, code):
         di, dj = code // 3 - 1, code % 3 - 1
         if di != 0 and dj != 0 and e not in DIRECT:
-            source = ghosts(ext, 3 * (di + 1) + 1)
+            source = ghosts(e, ext, 3 * (di + 1) + 1)
             target = (i, j - dj)
         else:
             target = (i - di, j - dj)
         return pltpu.make_async_remote_copy(
-            src_ref=source, dst_ref=ghosts(ext, code), send_sem=send_sem.at[e, code],
+            src_ref=source, dst_ref=ghosts(e, ext, code), send_sem=send_sem.at[e, code],
             recv_sem=recv_sem.at[e, code], device_id=target, device_id_type=MESH)
 
     def sends(e, code):
@@ -168,22 +175,25 @@
             parts += [part, part]
         return jnp.dot(jnp.concatenate(parts, axis=1), w[s], preferred_element_type=F32)
 
-    def viscous(s, _):
+    def ustar_of(s):
         out = apply(s, lambda n: split(jnp.concatenate([pos[n], mot[n]], axis=0)))
         out = out[0:8] + out[8:16]
-        sums[s] = out
         speed = mot[s]
         ustar = speed + 0.5 * (out[4:8] / out[7:8] - speed)
         both = pos[s] * ustar
         rows = jnp.concatenate([ustar[0:3], both[0:1] + both[1:2] + both[2:3]], axis=0)
-        flow[s] = rows
-        flow_own[s] = rows
-        return 0
-
-    lax.fori_loop(0, S, viscous, 0, unroll=4)
-
-    def stage_flow(g, _):
-        st_flow[g] = flow_own[send_ref[0, 0, g]]
+        return out, rows
+
+    def viscous(s, _):
+        sums[s], flow[s] = ustar_of(s)
+        return 0
+
+    def lend_early(g, _):
+        st_flow[g] = ustar_of(send_ref[0, 0, g])[1]
+        return 0
+
+    def lend_late(g, _):
+        st_late[g - half] = ustar_of(send_ref[0, 0, g])[1]
         return 0
 
     def exchange(e, ext, staged):
@@ -191,8 +201,16 @@
         forward(e, ext, staged)
         arrive(e, ext, staged)
 
-    lax.fori_loop(0, G, stage_flow, 0, unroll=8)
-    exchange(2, flow, st_flow)
+    lax.fori_loop(0, half, lend_early, 0, unroll=4)
+    begin(2, flow, st_flow)
+    lax.fori_loop(half, G, lend_late, 0, unroll=4)
+    begin(LATE, flow, st_late)
+    forward(2, flow, st_flow)
+    lax.fori_loop(0, S // 2, viscous, 0, unroll=8)
+    forward(LATE, flow, st_late)
+    lax.fori_loop(S // 2, S, viscous, 0, unroll=8)
+    arrive(2, flow, st_flow)
+    arrive(LATE, flow, st_late)
 
     def source(s, _):
         out = apply(s, lambda n: split(flow[n]))
@@ -207,7 +225,7 @@
         ztot[pl.ds(s, 1), :] = total
         return 0
 
-    lax.fori_loop(0, S, source, 0, unroll=4)
+    lax.fori_loop(0, S, source, 0, unroll=8)
 
     def precondition():
         def one(s, _):
@@ -244,7 +262,7 @@
                 mres[pl.ds(s, 1), :] = out[0:1] + out[1:2]
                 return 0
 
-            lax.fori_loop(0, S, operate, 0, unroll=4)
+            lax.fori_loop(0, S, operate, 0, unroll=8)
             src[...] = src[...] - (2.0 * step - mres[...] / ztot[...])
             rho_new = 1.0 / (2.0 * sigma - rho)
             step = rho_new * rho * step + 2.0 * rho_new / delta * precondition()
@@ -273,11 +291,12 @@
             vel_ref[0, 0, c, pl.ds(s, 1), :] = result[c:c + 1]
         return 0
 
-    lax.fori_loop(0, S, gradient, 0, unroll=4)
+    lax.fori_loop(0, S, gradient, 0, unroll=8)
 
     finish(0, pos, st_pos)
     finish(1, mot, st_mot)
     finish(2, flow, st_flow)
+    finish(LATE, flow, st_late)
     for it in range(ITERS):
         finish(3 + it, steps[it], st_step[it])
 
@@ -289,7 +308,7 @@
     N = S + 9 * G
     vmem = pl.BlockSpec(memory_space=pltpu.VMEM)
     smem = pl.BlockSpec(memory_space=pltpu.SMEM)
-    exchanges = 3 + ITERS
+    exchanges = 4 + ITERS
     swap = lambda array: jnp.swapaxes(array, 2, 3)
     press, vel = pl.pallas_call(
         functools.partial(kernel, px, py, (S, G, K, T)),
@@ -303,7 +322,6 @@
             pltpu.VMEM((N, 4, T), F32),
             pltpu.VMEM((N, 4, T), F32),
             pltpu.VMEM((N, 4, T), F32),
-            pltpu.VMEM((S, 4, T), F32),
             *[pltpu.VMEM((N, T), F32)] * ITERS,
             pltpu.VMEM((S, T), F32),
             pltpu.VMEM((N, T), F32),
@@ -313,7 +331,8 @@
             pltpu.VMEM((S, T), F32),
             pltpu.VMEM((G, 4, T), F32),
             pltpu.VMEM((G, 4, T), F32),
-            pltpu.VMEM((G, 4, T), F32),
+            pltpu.VMEM((G // 2, 4, T), F32),
+            pltpu.VMEM((G - G // 2, 4, T), F32),
             *[pltpu.VMEM((G, T), F32)] * ITERS,
             pltpu.SemaphoreType.DMA,
             pltpu.SemaphoreType.DMA((exchanges, 9)),

time: 63.6 us -> 60.6 us (0.953)
  Pallas kernels: 55.2 us -> 52.7 us
    pallas_call x1, Pallas kernels: 55.2 us -> 52.7 us  [body(): pl.pallas_call(functools.partial(kernel, px, py, (S, G, K, T)), out_shape...]
where the time goes in v2:
time: 60.6 us; the launch traced here: 60.3 us
  Pallas kernels  52.7 us (87%)
  local copies, waits for them, and re-layouts  5.07 us (8%)
  between operations  2.58 us (4%)
    pallas_call x1, Pallas kernels, body(): pl.pallas_call(functools.partial(kernel, px, py, (S, G, K, T)), out_shape...  52.7 us
    unnamed x8, local copies, waits for them, and re-layouts  4.36 us

profile of v2, /device:TPU:1, one launch (start us, length us, event | category | flops | bytes accessed | tf_op | source)
XLA Modules:
  0.0 60.3 jit_solution(6281807857440688597)
XLA Ops:
  2.6 0.7 %copy_bitcast_fusion = (s32[1,1,9,32]{3,2,1,0:T(8,128)S(1)}, s32[1,1,9,32]{3,2,1,0:T(8,128)S(1)}) fusion(s32[1,1,32,9]{2,1,3,0:T(1,128)} %param.15, s32[1,1,32,9]{2,1,3,0:T(1,128)} %param.14), kind=kLoop, calls=%fused_computation | loop fusion | bytes 4608 | tf_op jit(solution)/shard_map/transpose | solution.py:312
  3.3 0.0 copy-start
  3.3 1.6 %copy-done = f32[1,1,32,128,128]{4,3,2,1,0:T(8,128)S(1)} copy-done((f32[1,1,32,128,128]{4,3,2,1,0:T(8,128)S(1)}, f32[1,1,32,128,128]{4,3,2,1,0:T(8,128)}, u32[]{:S(2)}) %copy-start) | copy-done | bytes 2097176
  4.9 0.0 copy-start.1
  4.9 0.9 %copy-done.1 = f32[1,1,32,6,128]{4,2,3,1,0:T(8,128)S(1)} copy-done((f32[1,1,32,6,128]{4,2,3,1,0:T(8,128)S(1)}, f32[1,1,32,6,128]{4,2,3,1,0:T(8,128)}, u32[]{:S(2)}) %copy-start.1) | copy-done | bytes 98328
  5.8 0.0 copy-start.2
  5.8 0.7 %copy-done.2 = s32[1,1,24]{2,1,0:T(1,128)S(1)} copy-done((s32[1,1,24]{2,1,0:T(1,128)S(1)}, s32[1,1,24]{2,1,0:T(1,128)}, u32[]{:S(2)}) %copy-start.2) | copy-done | bytes 120
  6.4 52.7 %shard_map.95 = (f32[1,1,32,128]{3,2,1,0:T(8,128)S(1)}, f32[1,1,3,32,128]{4,3,2,1,0:T(8,128)S(1)}) custom-call(f32[1,1,6,32,128]{4,3,2,1,0:T(8,128)S(1)} %bitcast.6, f32[1,1,32,128,128]{4,3,2,1,0:T(8,128)S(1)} %copy-done, f32[1]{0:T(128)S(6)} %copy.16.low_ref, f32[1]{0:T(128)S(6)} %copy.17.high_ref, s32[1,1]{1,0:T(1,128)S(6)} %copy.18.counts_ref, ...), custom_call_target="tpu_custom_call" | custom-call | tf_op jit(solution)/shard_map/pallas_call | solution.py:313
  59.1 0.6 %copy.19 = f32[1,1,32,128]{3,2,1,0:T(8,128)} copy(f32[1,1,32,128]{3,2,1,0:T(8,128)S(1)} %get-tuple-element.10) | data formatting | bytes 32768
  59.7 0.6 %copy.20 = f32[1,1,32,3,128]{4,2,3,1,0:T(8,128)} copy(f32[1,1,32,3,128]{4,2,3,1,0:T(8,128)S(1)} %bitcast.7) | data formatting | bytes 98304
Async XLA Ops:
  3.3 1.6 %copy-start = (f32[1,1,32,128,128]{4,3,2,1,0:T(8,128)S(1)}, f32[1,1,32,128,128]{4,3,2,1,0:T(8,128)}, u32[]{:S(2)}) copy-start(f32[1,1,32,128,128]{4,3,2,1,0:T(8,128)} %dinv_ref.1) | copy-start | bytes 6291460
  4.9 0.9 %copy-start.1 = (f32[1,1,32,6,128]{4,2,3,1,0:T(8,128)S(1)}, f32[1,1,32,6,128]{4,2,3,1,0:T(8,128)}, u32[]{:S(2)}) copy-start(f32[1,1,32,6,128]{4,2,3,1,0:T(8,128)} %param.8) | copy-start | bytes 294916
  5.8 0.7 %copy-start.2 = (s32[1,1,24]{2,1,0:T(1,128)S(1)}, s32[1,1,24]{2,1,0:T(1,128)}, u32[]{:S(2)}) copy-start(s32[1,1,24]{2,1,0:T(1,128)} %send_ref.1) | copy-start | bytes 292
